TPU v7x, 128 devices: a whole 4x4x4 slice. The times are simulated.
128 devices in a mesh: circ: 16 (over z_hi, y, core), xsec: 8 (over z_lo, x).
Axes of the slice: x: 4, y: 4, z: 4 (z_hi: 2, z_lo: 2; z = z_hi * 2 + z_lo), core: 2. Of those that a mesh axis runs over, the one named last changes fastest.
Arguments:
- displacement: float32 [3, 6291456], P(None, ('circ', 'xsec')), may hold values from -2 to 2
- velocity: float32 [3, 6291456], P(None, ('circ', 'xsec')), may hold values from -2 to 2
- load: float32 [3, 6291456], P(None, ('circ', 'xsec')), may hold values from -3 to 3
- mass: float32 [6291456], P(('circ', 'xsec')), may hold values from 1 to 4
- stiffness: float32 [64, 64, 131072], P(None, None, ('circ', 'xsec')), may hold values from -0.4 to 4.5
- connectivity: int32 [64, 131072], P(None, ('circ', 'xsec')), may hold values from 0 to 51199, as said below
- clearance: float32 [16384, 128], P(('circ', 'xsec')), may hold values from -0.3 to 0.3
- match_device: int32 [4, 16384, 1], P(None, ('circ', 'xsec')), may hold values from 0 to 127; in each aligned block of 128 rows (0 to 127, 128 to 255, ..., all dimensions but the last counted through in order) at most 2 rows name the same one
- match_slot: int32 [4, 16384], P(None, ('circ', 'xsec')), may hold values from 0 to 127
Outputs:
- final_displacement: float32 [3, 6291456], P(None, ('circ', 'xsec'))
- final_velocity: float32 [3, 6291456], P(None, ('circ', 'xsec'))
Inputs may be any that keep to these rules, and one draw needn't show every extreme that they name: `match_device`: in every step, at most 2 of one device's 128 cycle blocks name the same device, and some device's blocks name one device exactly 2 times. `connectivity`: all nodes of one element block lie in one aligned run of 64 extended nodes (indices t * 64 to t * 64 + 63 for some t).
All inputs are finite; a program needn't handle non-finite values.
Results may differ from a plain program's by a relative error of at most 0.0001.
Values sent between devices are 32-bit elements; how exact they have to be, the bound alone decides.
A program may use at most 192 MiB of HBM per device.

v0:
```python
import jax
import jax.numpy as jnp
from jax import lax
from jax.sharding import PartitionSpec as P

FACE = 1024


PENALTY = 4.0
DASHPOT = 1.0
FRICTION = 2.0
TIMESTEP = 0.25


def with_halo(block, sides, width):
    for axis, dim in sides:
        count = lax.axis_size(axis)
        forward = [(i, i + 1) for i in range(count - 1)]
        forward.append((count - 1, 0))
        backward = [(target, source) for source, target in forward]
        low = lax.ppermute(
            lax.slice_in_dim(block, block.shape[dim] - width, None, axis=dim), axis, forward
        )
        high = lax.ppermute(lax.slice_in_dim(block, 0, width, axis=dim), axis, backward)
        block = jnp.concatenate([low, block, high], axis=dim)
    return block


def shifted(array, axis, by):
    length = lax.axis_size(axis)
    return lax.ppermute(array, axis, [(i, (i + by) % length) for i in range(length)])


def contact_terms(cycle_disp, cycle_move, groove_disp, groove_move, clear):
    relative = [cycle_disp[k] - groove_disp[k] for k in range(3)]
    intersection = jnp.maximum(relative[0] - clear, 0.0)
    closing = cycle_move[0] - groove_move[0]
    return [
        intersection * (PENALTY + DASHPOT * closing),
        FRICTION * intersection * relative[1],
        FRICTION * intersection * relative[2],
    ]


def contact_step(deform, motion, clearance, target_dev, target_slot):
    own = deform.shape[1]
    cycle_count = clearance.shape[0]
    contact_nodes = clearance.shape[1]
    surface = cycle_count * contact_nodes
    groove_start = own - surface
    circ_count = lax.axis_size("circ")
    devices = circ_count * lax.axis_size("xsec")
    capacity = max(2, 2 * cycle_count // devices)
    slots = devices * capacity
    order = jnp.arange(cycle_count)
    earlier = (target_dev[:, None] == target_dev[None, :]) & (order[None, :] < order[:, None])
    rank = jnp.sum(earlier.astype(jnp.int32), axis=1)
    position = target_dev * capacity + rank
    picked = jnp.arange(slots)[:, None] == position[None, :]
    pick_float = picked.astype(jnp.float32)
    pick_int = picked.astype(jnp.int32)
    cycle_data = jnp.concatenate([deform[:, :surface], motion[0:1, :surface]], axis=0).reshape(
        4, cycle_count, contact_nodes
    )
    outgoing = jnp.einsum("sb,kbn->skn", pick_float, cycle_data, precision=lax.Precision.HIGHEST)
    filled = jnp.sum(pick_int, axis=1)
    slot_ids = (jnp.sum(pick_int * target_slot[None, :], axis=1) + (1 - filled) * cycle_count)[
        :, None
    ]
    incoming, in_ids = (
        lax.all_to_all(outgoing, ("circ", "xsec"), split_axis=0, concat_axis=0, tiled=True),
        lax.all_to_all(slot_ids, ("circ", "xsec"), split_axis=0, concat_axis=0, tiled=True),
    )
    matched = (jnp.arange(cycle_count)[:, None] == in_ids[None, :, 0]).astype(jnp.float32)
    groove_data = jnp.concatenate(
        [deform[:, groove_start:], motion[:, groove_start:]], axis=0
    ).reshape(6, cycle_count, contact_nodes)
    groove_data = jnp.concatenate([groove_data, clearance[None]], axis=0)
    seen = jnp.einsum("bs,kbn->skn", matched, groove_data, precision=lax.Precision.HIGHEST)
    terms = contact_terms(
        [incoming[:, k] for k in range(3)],
        [incoming[:, 3]],
        [seen[:, k] for k in range(3)],
        [seen[:, 3 + k] for k in range(3)],
        seen[:, 6],
    )
    pair_force = jnp.stack(terms, axis=1)
    groove_force = jnp.einsum("bs,skn->kbn", matched, pair_force, precision=lax.Precision.HIGHEST)
    returned = lax.all_to_all(pair_force, ("circ", "xsec"), split_axis=0, concat_axis=0, tiled=True)
    cycle_force = -jnp.einsum("sb,skn->kbn", pick_float, returned, precision=lax.Precision.HIGHEST)
    contact = jnp.zeros((3, own), jnp.float32)
    contact = contact.at[:, :surface].add(cycle_force.reshape(3, surface))
    contact = contact.at[:, groove_start:].add(groove_force.reshape(3, surface))
    return contact


def body(
    displacement, velocity, load, mass, stiffness, connectivity, clearance, match_device, match_slot
):
    own = displacement.shape[1]
    face = FACE
    width = stiffness.shape[0]
    tile_count = (own + 2 * face) // width
    tile_of = connectivity[0] // width
    local_of = connectivity % width
    tile_pick = (tile_of[:, None] == jnp.arange(tile_count)[None, :]).astype(jnp.float32)
    local_pick = (local_of[:, None, :] == jnp.arange(width)[None, :, None]).astype(jnp.float32)
    deform = displacement
    motion = velocity
    for step_index in range(match_slot.shape[0]):
        extended = with_halo(deform, (("circ", 1),), face)
        tiles = extended.reshape(3, tile_count, width)
        block_tile = jnp.einsum("et,ctm->cme", tile_pick, tiles, precision=lax.Precision.HIGHEST)
        gathered = jnp.einsum(
            "jme,cme->cje", local_pick, block_tile, precision=lax.Precision.HIGHEST
        )
        product = jnp.einsum("ije,cje->cie", stiffness, gathered, precision=lax.Precision.HIGHEST)
        spread = jnp.einsum("ime,cie->cme", local_pick, product, precision=lax.Precision.HIGHEST)
        summed = jnp.einsum(
            "et,cme->ctm", tile_pick, spread, precision=lax.Precision.HIGHEST
        ).reshape(3, own + 2 * face)
        internal = summed[:, face : face + own]
        from_upper = shifted(summed[:, :face], "circ", -1)
        from_lower = shifted(summed[:, face + own :], "circ", 1)
        internal = internal.at[:, own - face :].add(from_upper)
        internal = internal.at[:, :face].add(from_lower)
        contact = contact_step(
            deform, motion, clearance, match_device[step_index, :, 0], match_slot[step_index]
        )
        accel = (load - internal + contact) / mass[None, :]
        motion = motion + TIMESTEP * accel
        deform = deform + TIMESTEP * motion
    return (deform, motion)


def solution(mesh):
    return jax.shard_map(
        body,
        mesh=mesh,
        in_specs=(
            P(None, ("circ", "xsec")),
            P(None, ("circ", "xsec")),
            P(None, ("circ", "xsec")),
            P(("circ", "xsec")),
            P(None, None, ("circ", "xsec")),
            P(None, ("circ", "xsec")),
            P(("circ", "xsec"), None),
            P(None, ("circ", "xsec"), None),
            P(None, ("circ", "xsec")),
        ),
        out_specs=(P(None, ("circ", "xsec")), P(None, ("circ", "xsec"))),
        check_vma=False,
    )
```

profile of v0, /device:TPU:36, one launch (start us, length us, event | category | flops | bytes accessed | tf_op | source)
XLA Modules:
  0.0 816.8 jit_solution(13700131795126388127)
XLA Ops:
  4.3 10.2 %all-to-all-start.1 = ((s32[128,2,1]{1,2,0:T(1,128)}), s32[128,2,1]{1,2,0:T(1,128)S(1)}, u32[]{:S(2)}, u32[]{:S(2)}) async-start(s32[128,2,1]{1,2,0:T(1,128)} %bitcast.9), calls=%async_computation.1 | async-start | bytes 131072 | tf_op jit(solution)/shard_map/all_to_all | solution.py:72
  26.3 30.7 %copy.119 = f32[64,64,1024]{1,0,2:T(8,128)} copy(f32[64,64,1024]{2,1,0:T(8,128)} %param.45) | data formatting | bytes 33554432 | tf_op args[4]
  76.2 29.9 %fusion.7 = f32[1024,3,64]{2,1,0:T(4,128)S(1)} fusion(f32[3,64,1024]{1,0,2:T(4,128)} %copy.118, s32[64,1024]{0,1:T(8,128)S(1)} %copy.117), kind=kOutput, calls=%fused_computation.8 | convolution fusion | flops 155189248 | bytes 1835008 | tf_op jit(solution)/shard_map/jme,cme->cje/dot_general | solution.py:114
  106.1 56.7 %fusion.43 = f32[1024,3,64]{2,1,0:T(4,128)} fusion(f32[64,64,1024]{1,0,2:T(8,128)} %copy.119, f32[1024,3,64]{2,1,0:T(4,128)S(1)} %fusion.7), kind=kOutput, calls=%fused_computation.37 | convolution fusion | flops 150994944 | bytes 18350080 | tf_op jit(solution)/shard_map/ije,cje->cie/dot_general | solution.py:117
  162.8 9.8 %all-to-all-start.7 = ((s32[128,2,1]{1,2,0:T(1,128)}), s32[128,2,1]{1,2,0:T(1,128)S(1)}, u32[]{:S(2)}, u32[]{:S(2)}) async-start(s32[128,2,1]{1,2,0:T(1,128)} %bitcast.34), calls=%async_computation.7 | async-start | bytes 131072 | tf_op jit(solution)/shard_map/all_to_all | solution.py:72
  172.6 22.1 %fusion.53 = f32[3,64,1024]{1,0,2:T(4,128)} fusion(s32[64,1024]{0,1:T(8,128)S(1)} %copy.117, f32[1024,3,64]{2,1,0:T(4,128)} %fusion.43), kind=kOutput, calls=%fused_computation.47 | convolution fusion | flops 155189248 | bytes 1835008 | tf_op jit(solution)/shard_map/ime,cie->cme/dot_general | solution.py:118
  194.7 9.8 %all-to-all-start.10 = ((s32[128,2,1]{1,2,0:T(1,128)}), s32[128,2,1]{1,2,0:T(1,128)S(1)}, u32[]{:S(2)}, u32[]{:S(2)}) async-start(s32[128,2,1]{1,2,0:T(1,128)} %bitcast.46), calls=%async_computation.10 | async-start | bytes 131072 | tf_op jit(solution)/shard_map/all_to_all | solution.py:72
  213.1 9.8 %all-to-all-start = ((f32[256,4,128]{2,1,0:T(4,128)}), f32[256,4,128]{2,1,0:T(4,128)S(1)}, u32[]{:S(2)}, u32[]{:S(2)}) async-start(f32[256,4,128]{2,1,0:T(4,128)} %copy.122), calls=%async_computation | async-start | bytes 1048576 | tf_op jit(solution)/shard_map/all_to_all | solution.py:71
  237.9 10.2 %all-to-all-start.2 = ((f32[256,3,128]{2,1,0:T(4,128)}), f32[256,3,128]{2,1,0:T(4,128)S(1)}, u32[]{:S(2)}, u32[]{:S(2)}) async-start(f32[256,3,128]{2,1,0:T(4,128)} %copy.129), calls=%async_computation.2 | async-start | bytes 1048576 | tf_op jit(solution)/shard_map/all_to_all | solution.py:89
  251.2 8.0 all-to-all-done.2
  289.1 29.9 %fusion.5 = f32[1024,3,64]{2,1,0:T(4,128)S(1)} fusion(f32[3,64,1024]{1,0,2:T(4,128)} %copy.135, s32[64,1024]{0,1:T(8,128)S(1)} %copy-done.25), kind=kOutput, calls=%fused_computation.6 | convolution fusion | flops 155189248 | bytes 1835008 | tf_op jit(solution)/shard_map/jme,cme->cje/dot_general | solution.py:114
  319.0 55.9 %fusion.40 = f32[1024,3,64]{2,1,0:T(4,128)S(1)} fusion(f32[64,64,1024]{1,0,2:T(8,128)} %copy.119, f32[1024,3,64]{2,1,0:T(4,128)S(1)} %fusion.5), kind=kOutput, calls=%fused_computation.34 | convolution fusion | flops 150994944 | bytes 18350080 | tf_op jit(solution)/shard_map/ije,cje->cie/dot_general | solution.py:117
  374.9 23.8 %fusion.56 = f32[3,64,1024]{1,0,2:T(4,128)S(1)} fusion(s32[64,1024]{0,1:T(8,128)S(1)} %copy-done.25, f32[1024,3,64]{2,1,0:T(4,128)S(1)} %fusion.40), kind=kOutput, calls=%fused_computation.48 | convolution fusion | flops 155189248 | bytes 1835008 | tf_op jit(solution)/shard_map/ime,cie->cme/dot_general | solution.py:118
  421.4 10.0 %all-to-all-start.5 = ((f32[256,3,128]{2,1,0:T(4,128)}), f32[256,3,128]{2,1,0:T(4,128)S(1)}, u32[]{:S(2)}, u32[]{:S(2)}) async-start(f32[256,3,128]{2,1,0:T(4,128)} %copy.146), calls=%async_computation.5 | async-start | bytes 1048576 | tf_op jit(solution)/shard_map/all_to_all | solution.py:89
  434.3 8.3 %all-to-all-done.5 = f32[256,3,128]{2,1,0:T(4,128)S(1)} async-done(((f32[256,3,128]{2,1,0:T(4,128)}), f32[256,3,128]{2,1,0:T(4,128)S(1)}, u32[]{:S(2)}, u32[]{:S(2)}) %all-to-all-start.5) | async-done | bytes 393248 | tf_op jit(solution)/shard_map/all_to_all | solution.py:89
  456.3 7.6 all-to-all-start.6
  470.6 29.9 %fusion.3 = f32[1024,3,64]{2,1,0:T(4,128)S(1)} fusion(f32[3,64,1024]{1,0,2:T(4,128)} %copy.152, s32[64,1024]{0,1:T(8,128)S(1)} %copy-done.26), kind=kOutput, calls=%fused_computation.4 | convolution fusion | flops 155189248 | bytes 1835008 | tf_op jit(solution)/shard_map/jme,cme->cje/dot_general | solution.py:114
  500.5 55.7 %fusion.37 = f32[1024,3,64]{2,1,0:T(4,128)S(1)} fusion(f32[64,64,1024]{1,0,2:T(8,128)} %copy.119, f32[1024,3,64]{2,1,0:T(4,128)S(1)} %fusion.3), kind=kOutput, calls=%fused_computation.31 | convolution fusion | flops 150994944 | bytes 18350080 | tf_op jit(solution)/shard_map/ije,cje->cie/dot_general | solution.py:117
  556.2 23.8 %fusion.59 = f32[3,64,1024]{1,0,2:T(4,128)S(1)} fusion(s32[64,1024]{0,1:T(8,128)S(1)} %copy-done.26, f32[1024,3,64]{2,1,0:T(4,128)S(1)} %fusion.37), kind=kOutput, calls=%fused_computation.49 | convolution fusion | flops 155189248 | bytes 1835008 | tf_op jit(solution)/shard_map/ime,cie->cme/dot_general | solution.py:118
  600.6 10.4 %all-to-all-start.8 = ((f32[256,3,128]{2,1,0:T(4,128)}), f32[256,3,128]{2,1,0:T(4,128)}, u32[]{:S(2)}, u32[]{:S(2)}) async-start(f32[256,3,128]{2,1,0:T(4,128)} %copy.163), calls=%async_computation.8 | async-start | bytes 1048576 | tf_op jit(solution)/shard_map/all_to_all | solution.py:89
  654.7 29.9 %fusion.1 = f32[1024,3,64]{2,1,0:T(4,128)S(1)} fusion(f32[3,64,1024]{1,0,2:T(4,128)} %copy.169, s32[64,1024]{0,1:T(8,128)S(1)} %copy-done.27), kind=kOutput, calls=%fused_computation.2 | convolution fusion | flops 155189248 | bytes 1835008 | tf_op jit(solution)/shard_map/jme,cme->cje/dot_general | solution.py:114
  684.6 55.7 %fusion.34 = f32[1024,3,64]{2,1,0:T(4,128)S(1)} fusion(f32[64,64,1024]{1,0,2:T(8,128)} %copy.119, f32[1024,3,64]{2,1,0:T(4,128)S(1)} %fusion.1), kind=kOutput, calls=%fused_computation.28 | convolution fusion | flops 150994944 | bytes 18350080 | tf_op jit(solution)/shard_map/ije,cje->cie/dot_general | solution.py:117
  740.3 23.6 %fusion.62 = f32[3,64,1024]{1,0,2:T(4,128)S(1)} fusion(s32[64,1024]{0,1:T(8,128)S(1)} %copy-done.27, f32[1024,3,64]{2,1,0:T(4,128)S(1)} %fusion.34), kind=kOutput, calls=%fused_computation.50 | convolution fusion | flops 155189248 | bytes 1835008 | tf_op jit(solution)/shard_map/ime,cie->cme/dot_general | solution.py:118
  786.6 10.4 %all-to-all-start.11 = ((f32[256,3,128]{2,1,0:T(4,128)}), f32[256,3,128]{2,1,0:T(4,128)}, u32[]{:S(2)}, u32[]{:S(2)}) async-start(f32[256,3,128]{2,1,0:T(4,128)} %copy.180), calls=%async_computation.11 | async-start | bytes 1048576 | tf_op jit(solution)/shard_map/all_to_all | solution.py:89
  (302 shorter events, 242.6 us)
Async XLA Ops:
  4.3 56.3 %all-to-all-start.1 = ((s32[128,2,1]{1,2,0:T(1,128)}), s32[128,2,1]{1,2,0:T(1,128)S(1)}, u32[]{:S(2)}, u32[]{:S(2)}) async-start(s32[128,2,1]{1,2,0:T(1,128)} %bitcast.9), calls=%async_computation.1 | async-start | bytes 131072 | tf_op jit(solution)/shard_map/all_to_all | solution.py:72
  15.3 54.5 %collective-permute-start = (f32[3,1024]{1,0:T(4,128)S(1)}, f32[3,1024]{1,0:T(4,128)S(1)}, u32[]{:S(2)}, u32[]{:S(2)}) collective-permute-start(f32[3,1024]{1,0:T(4,128)S(1)} %get-tuple-element.246), channel_id=1, source_target_pairs={{0,8},{8,16},{16,24},{24,32},{32,40},{40,48},{48,56},{56,64},{64,7... | collective-permute-start | bytes 36872 | tf_op jit(solution)/shard_map/ppermute | solution.py:21
  15.4 54.4 %collective-permute-start.1 = (f32[3,1024]{1,0:T(4,128)S(1)}, f32[3,1024]{1,0:T(4,128)S(1)}, u32[]{:S(2)}, u32[]{:S(2)}) collective-permute-start(f32[3,1024]{1,0:T(4,128)S(1)} %get-tuple-element.247), channel_id=1, source_target_pairs={{8,0},{16,8},{24,16},{32,24},{40,32},{48,40},{56,48},{64,56},{72,6... | collective-permute-start | bytes 36872 | tf_op jit(solution)/shard_map/ppermute | solution.py:24
  60.6 102.2 %all-to-all-start.4 = ((s32[128,2,1]{1,2,0:T(1,128)}), s32[128,2,1]{1,2,0:T(1,128)S(1)}, u32[]{:S(2)}, u32[]{:S(2)}) async-start(s32[128,2,1]{1,2,0:T(1,128)} %bitcast.22), calls=%async_computation.4 | async-start | bytes 131072 | tf_op jit(solution)/shard_map/all_to_all | solution.py:72
  162.8 31.9 %all-to-all-start.7 = ((s32[128,2,1]{1,2,0:T(1,128)}), s32[128,2,1]{1,2,0:T(1,128)S(1)}, u32[]{:S(2)}, u32[]{:S(2)}) async-start(s32[128,2,1]{1,2,0:T(1,128)} %bitcast.34), calls=%async_computation.7 | async-start | bytes 131072 | tf_op jit(solution)/shard_map/all_to_all | solution.py:72
  194.7 18.4 %all-to-all-start.10 = ((s32[128,2,1]{1,2,0:T(1,128)}), s32[128,2,1]{1,2,0:T(1,128)S(1)}, u32[]{:S(2)}, u32[]{:S(2)}) async-start(s32[128,2,1]{1,2,0:T(1,128)} %bitcast.46), calls=%async_computation.10 | async-start | bytes 131072 | tf_op jit(solution)/shard_map/all_to_all | solution.py:72
  213.1 21.2 %all-to-all-start = ((f32[256,4,128]{2,1,0:T(4,128)}), f32[256,4,128]{2,1,0:T(4,128)S(1)}, u32[]{:S(2)}, u32[]{:S(2)}) async-start(f32[256,4,128]{2,1,0:T(4,128)} %copy.122), calls=%async_computation | async-start | bytes 1048576 | tf_op jit(solution)/shard_map/all_to_all | solution.py:71
  234.2 14.0 %collective-permute-start.3 = (f32[3,1024]{1,0:T(4,128)}, f32[3,1024]{1,0:T(4,128)S(1)}, u32[]{:S(2)}, u32[]{:S(2)}) collective-permute-start(f32[3,1024]{1,0:T(4,128)} %get-tuple-element.232), channel_id=1, source_target_pairs={{0,8},{8,16},{16,24},{24,32},{32,40},{40,48},{48,56},{56,64},{64,7... | collective-permute-start | bytes 36872 | tf_op jit(solution)/shard_map/ppermute | solution.py:31
  237.9 21.3 %all-to-all-start.2 = ((f32[256,3,128]{2,1,0:T(4,128)}), f32[256,3,128]{2,1,0:T(4,128)S(1)}, u32[]{:S(2)}, u32[]{:S(2)}) async-start(f32[256,3,128]{2,1,0:T(4,128)} %copy.129), calls=%async_computation.2 | async-start | bytes 1048576 | tf_op jit(solution)/shard_map/all_to_all | solution.py:89
  265.2 15.6 %collective-permute-start.4 = (f32[3,1024]{1,0:T(4,128)S(1)}, f32[3,1024]{1,0:T(4,128)S(1)}, u32[]{:S(2)}, u32[]{:S(2)}) collective-permute-start(f32[3,1024]{1,0:T(4,128)S(1)} %get-tuple-element.242), channel_id=1, source_target_pairs={{0,8},{8,16},{16,24},{24,32},{32,40},{40,48},{48,56},{56,64},{64,7... | collective-permute-start | bytes 36872 | tf_op jit(solution)/shard_map/ppermute | solution.py:21
  265.3 15.5 %collective-permute-start.5 = (f32[3,1024]{1,0:T(4,128)S(1)}, f32[3,1024]{1,0:T(4,128)S(1)}, u32[]{:S(2)}, u32[]{:S(2)}) collective-permute-start(f32[3,1024]{1,0:T(4,128)S(1)} %get-tuple-element.243), channel_id=1, source_target_pairs={{8,0},{16,8},{24,16},{32,24},{40,32},{48,40},{56,48},{64,56},{72,6... | collective-permute-start | bytes 36872 | tf_op jit(solution)/shard_map/ppermute | solution.py:24
  273.2 142.6 %all-to-all-start.3 = ((f32[256,4,128]{2,1,0:T(4,128)}), f32[256,4,128]{2,1,0:T(4,128)}, u32[]{:S(2)}, u32[]{:S(2)}) async-start(f32[256,4,128]{2,1,0:T(4,128)} %copy.139), calls=%async_computation.3 | async-start | bytes 1048576 | tf_op jit(solution)/shard_map/all_to_all | solution.py:71
  415.8 15.6 %collective-permute-start.7 = (f32[3,1024]{1,0:T(4,128)S(1)}, f32[3,1024]{1,0:T(4,128)S(1)}, u32[]{:S(2)}, u32[]{:S(2)}) collective-permute-start(f32[3,1024]{1,0:T(4,128)S(1)} %get-tuple-element.230), channel_id=1, source_target_pairs={{0,8},{8,16},{16,24},{24,32},{32,40},{40,48},{48,56},{56,64},{64,7... | collective-permute-start | bytes 36872 | tf_op jit(solution)/shard_map/ppermute | solution.py:31
  421.4 21.2 %all-to-all-start.5 = ((f32[256,3,128]{2,1,0:T(4,128)}), f32[256,3,128]{2,1,0:T(4,128)S(1)}, u32[]{:S(2)}, u32[]{:S(2)}) async-start(f32[256,3,128]{2,1,0:T(4,128)} %copy.146), calls=%async_computation.5 | async-start | bytes 1048576 | tf_op jit(solution)/shard_map/all_to_all | solution.py:89
  448.1 15.8 %collective-permute-start.8 = (f32[3,1024]{1,0:T(4,128)S(1)}, f32[3,1024]{1,0:T(4,128)S(1)}, u32[]{:S(2)}, u32[]{:S(2)}) collective-permute-start(f32[3,1024]{1,0:T(4,128)S(1)} %get-tuple-element.238), channel_id=1, source_target_pairs={{0,8},{8,16},{16,24},{24,32},{32,40},{40,48},{48,56},{56,64},{64,7... | collective-permute-start | bytes 36872 | tf_op jit(solution)/shard_map/ppermute | solution.py:21
  448.2 15.7 %collective-permute-start.9 = (f32[3,1024]{1,0:T(4,128)S(1)}, f32[3,1024]{1,0:T(4,128)S(1)}, u32[]{:S(2)}, u32[]{:S(2)}) collective-permute-start(f32[3,1024]{1,0:T(4,128)S(1)} %get-tuple-element.239), channel_id=1, source_target_pairs={{8,0},{16,8},{24,16},{32,24},{40,32},{48,40},{56,48},{64,56},{72,6... | collective-permute-start | bytes 36872 | tf_op jit(solution)/shard_map/ppermute | solution.py:24
  456.3 138.7 %all-to-all-start.6 = ((f32[256,4,128]{2,1,0:T(4,128)}), f32[256,4,128]{2,1,0:T(4,128)}, u32[]{:S(2)}, u32[]{:S(2)}) async-start(f32[256,4,128]{2,1,0:T(4,128)} %copy.156), calls=%async_computation.6 | async-start | bytes 1048576 | tf_op jit(solution)/shard_map/all_to_all | solution.py:71
  594.9 16.1 %collective-permute-start.11 = (f32[3,1024]{1,0:T(4,128)S(1)}, f32[3,1024]{1,0:T(4,128)S(1)}, u32[]{:S(2)}, u32[]{:S(2)}) collective-permute-start(f32[3,1024]{1,0:T(4,128)S(1)} %get-tuple-element.228), channel_id=1, source_target_pairs={{0,8},{8,16},{16,24},{24,32},{32,40},{40,48},{48,56},{56,64},{64,7... | collective-permute-start | bytes 36872 | tf_op jit(solution)/shard_map/ppermute | solution.py:31
  600.6 21.3 %all-to-all-start.8 = ((f32[256,3,128]{2,1,0:T(4,128)}), f32[256,3,128]{2,1,0:T(4,128)}, u32[]{:S(2)}, u32[]{:S(2)}) async-start(f32[256,3,128]{2,1,0:T(4,128)} %copy.163), calls=%async_computation.8 | async-start | bytes 1048576 | tf_op jit(solution)/shard_map/all_to_all | solution.py:89
  630.6 15.8 %collective-permute-start.12 = (f32[3,1024]{1,0:T(4,128)S(1)}, f32[3,1024]{1,0:T(4,128)S(1)}, u32[]{:S(2)}, u32[]{:S(2)}) collective-permute-start(f32[3,1024]{1,0:T(4,128)S(1)} %get-tuple-element.234), channel_id=1, source_target_pairs={{0,8},{8,16},{16,24},{24,32},{32,40},{40,48},{48,56},{56,64},{64,7... | collective-permute-start | bytes 36872 | tf_op jit(solution)/shard_map/ppermute | solution.py:21
  630.7 15.7 %collective-permute-start.13 = (f32[3,1024]{1,0:T(4,128)S(1)}, f32[3,1024]{1,0:T(4,128)S(1)}, u32[]{:S(2)}, u32[]{:S(2)}) collective-permute-start(f32[3,1024]{1,0:T(4,128)S(1)} %get-tuple-element.235), channel_id=1, source_target_pairs={{8,0},{16,8},{24,16},{32,24},{40,32},{48,40},{56,48},{64,56},{72,6... | collective-permute-start | bytes 36872 | tf_op jit(solution)/shard_map/ppermute | solution.py:24
  638.8 142.2 %all-to-all-start.9 = ((f32[256,4,128]{2,1,0:T(4,128)}), f32[256,4,128]{2,1,0:T(4,128)}, u32[]{:S(2)}, u32[]{:S(2)}) async-start(f32[256,4,128]{2,1,0:T(4,128)} %copy.173), calls=%async_computation.9 | async-start | bytes 1048576 | tf_op jit(solution)/shard_map/all_to_all | solution.py:71
  781.0 16.0 %collective-permute-start.15 = (f32[3,1024]{1,0:T(4,128)S(1)}, f32[3,1024]{1,0:T(4,128)S(1)}, u32[]{:S(2)}, u32[]{:S(2)}) collective-permute-start(f32[3,1024]{1,0:T(4,128)S(1)} %get-tuple-element.226), channel_id=1, source_target_pairs={{0,8},{8,16},{16,24},{24,32},{32,40},{40,48},{48,56},{56,64},{64,7... | collective-permute-start | bytes 36872 | tf_op jit(solution)/shard_map/ppermute | solution.py:31
  786.6 21.3 %all-to-all-start.11 = ((f32[256,3,128]{2,1,0:T(4,128)}), f32[256,3,128]{2,1,0:T(4,128)}, u32[]{:S(2)}, u32[]{:S(2)}) async-start(f32[256,3,128]{2,1,0:T(4,128)} %copy.180), calls=%async_computation.11 | async-start | bytes 1048576 | tf_op jit(solution)/shard_map/all_to_all | solution.py:89
  (51 other events, 795.3 us)
where the time goes:
time: 830 us; the launch traced here: 817 us
  matrix products  498 us (60%)
  starting transfers between devices  151 us (18%)
  local copies, waits for them, and re-layouts  108 us (13%)
  other arithmetic  29.5 us (4%)
  waiting for transfers between devices  28.5 us (3%)
    dot_general x4, matrix products, body(): jnp.einsum('ije,cje->cie', stiffness, gathered, precision=lax.Precision.H...  224 us
    dot_general x4, matrix products, body(): jnp.einsum('jme,cme->cje', local_pick, block_tile, precision=lax.Precisio...  119 us
    dot_general x4, matrix products, body(): jnp.einsum('ime,cie->cme', local_pick, product, precision=lax.Precision.H...  93.3 us
    all_to_all x4, starting transfers between devices, contact_step(): lax.all_to_all(pair_force, ('circ', 'xsec'), split_axis=0, concat_axis=0,...  41 us
    unnamed x93, local copies, waits for them, and re-layouts  37.2 us
    all_to_all x4, starting transfers between devices, contact_step(): lax.all_to_all(slot_ids, ('circ', 'xsec'), split_axis=0, concat_axis=0, t...  36.9 us
    all_to_all x4, starting transfers between devices, contact_step(): lax.all_to_all(outgoing, ('circ', 'xsec'), split_axis=0, concat_axis=0, t...  32.4 us
    all_to_all x4, waiting for transfers between devices, contact_step(): lax.all_to_all(pair_force, ('circ', 'xsec'), split_axis=0, concat_axis=0,...  28.4 us
  transfers between devices with their start and end apart: 28, of which 4 were waited for; matrix products, arithmetic and copies ran while one was open for 74% of the time, Pallas kernels for 0%

commit v1 on v0

v1 whole, which is shorter than its diff:
```python
import functools

import jax
import jax.numpy as jnp
from jax import lax
from jax.experimental import pallas as pl
from jax.experimental.pallas import tpu as pltpu
from jax.sharding import PartitionSpec as P

FACE = 1024
WIDTH = 64
LANES = 128
ROWS = 16
PENALTY = 4.0
DASHPOT = 1.0
FRICTION = 2.0
TIMESTEP = 0.25
BF16 = jnp.bfloat16
F32 = jnp.float32
MESH = pl.DeviceIdType.MESH


def parts(x):
    first = x.astype(BF16)
    rest = x - first.astype(F32)
    second = rest.astype(BF16)
    third = (rest - second.astype(F32)).astype(BF16)
    return first, second, third


def one_hot(mask):
    return jnp.where(mask, 1.0, 0.0).astype(BF16)


def dot(a, b):
    return jnp.dot(a, b, preferred_element_type=F32)


def iota(shape, dim):
    return lax.broadcasted_iota(jnp.int32, shape, dim)


def padded_transpose(block):
    rows = block.shape[0]
    return jnp.concatenate([block, jnp.zeros((LANES - rows, LANES), F32)], axis=0).T


def contact_terms(cycle, groove):
    relative = [cycle[k] - groove[k] for k in range(3)]
    intersection = jnp.maximum(relative[0], 0.0)
    closing = cycle[3] - groove[3]
    return [
        intersection * (PENALTY + DASHPOT * closing),
        FRICTION * intersection * relative[1],
        FRICTION * intersection * relative[2],
    ]


def column_of(block, own_blocks, face_blocks):
    upper = own_blocks + face_blocks
    return jnp.where(
        block < face_blocks,
        block + own_blocks,
        jnp.where(block >= upper, block + 2 * face_blocks, block - face_blocks),
    )


def fill_tables(conn_ref, column_ref, pick_ref, back_ref, own_blocks, face_blocks):
    groups = conn_ref.shape[0]
    columns = pick_ref.shape[0]
    for group in range(groups):
        row = column_of(conn_ref[group, 0:1, :] >> 7, own_blocks, face_blocks)
        pick_ref[:, group * LANES : (group + 1) * LANES] = one_hot(iota((columns, LANES), 0) == row)
        col = column_of(column_ref[:, group : group + 1] >> 7, own_blocks, face_blocks)
        back_ref[group * LANES : (group + 1) * LANES, :] = one_hot(iota((LANES, columns), 1) == col)


def gather_tiles(state_ref, pick_ref, tile_ref):
    groups = tile_ref.shape[0]
    for pair in range(groups // 2):
        pick = pick_ref[:, pair * 256 : (pair + 1) * 256]
        found = sum(dot(state_ref[p], pick) for p in range(3))
        tile_ref[2 * pair] = found[:, :LANES]
        tile_ref[2 * pair + 1] = found[:, LANES:]


def element_group(group, stiff_ref, conn_ref, tile_ref, near_ref, spread_ref):
    links = conn_ref[group]
    odd = ((links[0:1, :] >> 6) & 1) == 1
    low = links & 7
    high = (links >> 3) & 7
    for c in range(3):
        tile = jnp.where(
            odd,
            tile_ref[group, c * 128 + 64 : c * 128 + 128, :],
            tile_ref[group, c * 128 : c * 128 + 64, :],
        )
        for j in range(8):
            index = low[j * 8 : j * 8 + 8]
            which = high[j * 8 : j * 8 + 8]
            value = jnp.take_along_axis(tile[0:8], index, axis=0, mode="promise_in_bounds")
            for m in range(1, 8):
                other = jnp.take_along_axis(
                    tile[m * 8 : m * 8 + 8], index, axis=0, mode="promise_in_bounds"
                )
                value = jnp.where(which == m, other, value)
            near_ref[c, j * 8 : j * 8 + 8, :] = value

    def row(i, sums):
        stiff = stiff_ref[group, i]
        hit = iota((WIDTH, LANES), 0) == (conn_ref[group, pl.ds(i, 1), :] & 63)
        out = []
        for c in range(3):
            force = jnp.sum(stiff * near_ref[c], axis=0, keepdims=True)
            out.append(sums[c] + jnp.where(hit, force, 0.0))
        return tuple(out)

    zero = jnp.zeros((WIDTH, LANES), F32)
    sums = lax.fori_loop(0, WIDTH, row, (zero, zero, zero))
    at = pl.ds(pl.multiple_of(group * LANES, LANES), LANES)
    for c in range(3):
        for half in range(2):
            kept = jnp.where(odd if half else jnp.logical_not(odd), sums[c], 0.0)
            for p, part in enumerate(parts(kept)):
                spread_ref[p, c * 128 + half * 64 : c * 128 + half * 64 + 64, at] = part


def kernel(
    counts, disp_in, vel_in, load_ref, mass_ref, stiff_hbm, conn_ref, column_ref, clear_ref,
    target_ref, slot_ref, disp_ref, vel_ref,
    stiff_ref, pick_ref, back_ref, tile_ref, near_ref, spread_ref, state_ref, force_ref, scale_ref,
    pickers, pickers_t, seers, seers_t, note_out, note_in, send_ref, recv_ref,
    face_out, face_in, edge_out, edge_in,
    stiff_sem, note_send, note_recv, block_send, block_recv, face_send, face_recv, edge_send,
    edge_recv,
):
    circ_count, xsec_count, steps, own_blocks, face_blocks = counts
    devices = circ_count * xsec_count
    groups = stiff_ref.shape[0]
    circ, xsec = lax.axis_index("circ"), lax.axis_index("xsec")
    me = circ * xsec_count + xsec
    lower = (lax.rem(circ + circ_count - 1, circ_count), xsec)
    upper = (lax.rem(circ + 1, circ_count), xsec)

    def peer(r):
        other = lax.rem(me + r, devices)
        return other, (other // xsec_count, lax.rem(other, xsec_count))

    copies = [
        pltpu.make_async_copy(
            stiff_hbm.at[:, :, pl.ds(g * LANES, LANES)], stiff_ref.at[g], stiff_sem.at[g]
        )
        for g in range(groups)
    ]
    for copy in copies:
        copy.start()

    barrier = pltpu.get_barrier_semaphore()

    def greet(r, carry):
        pl.semaphore_signal(barrier, inc=1, device_id=peer(r)[1], device_id_type=MESH)
        return carry

    lax.fori_loop(1, devices, greet, 0)

    square = (LANES, LANES)
    note = jnp.zeros(square, F32)
    for s in range(steps):
        dev_row = target_ref[s : s + 1, :]
        dev_square = jnp.broadcast_to(dev_row, square)
        dev_col = dev_square.astype(F32).T.astype(jnp.int32)
        earlier = (dev_col == dev_square) & (iota(square, 0) < iota(square, 1))
        rank_row = jnp.sum(jnp.where(earlier, 1.0, 0.0), axis=0, keepdims=True).astype(jnp.int32)
        code_row = jnp.broadcast_to(dev_row + rank_row * devices, square)
        code_col = code_row.astype(F32).T.astype(jnp.int32)
        for r in range(2):
            mine = code_row == iota(square, 0) + r * devices
            pickers[s, r * LANES : (r + 1) * LANES, :] = one_hot(mine)
            pickers_t[s, :, r * LANES : (r + 1) * LANES] = one_hot(
                code_col == iota(square, 1) + r * devices
            )
            named = jnp.where(mine, (slot_ref[s : s + 1, :] + 1).astype(F32), 0.0)
            named = jnp.sum(named, axis=1, keepdims=True)
            note = note + jnp.where(iota(square, 1) == 2 * s + r, named, 0.0)
    note_out[...] = jnp.zeros(note_out.shape, F32)
    note_out[pl.ds(0, LANES, stride=8), :] = note

    pl.semaphore_wait(barrier, devices - 1)

    def tell(r, carry):
        other, where = peer(r)
        pltpu.make_async_remote_copy(
            src_ref=note_out.at[pl.ds(pl.multiple_of(other * 8, 8), 8)],
            dst_ref=note_in.at[pl.ds(pl.multiple_of(me * 8, 8), 8)],
            send_sem=note_send,
            recv_sem=note_recv,
            device_id=where,
            device_id_type=MESH,
        ).start()
        return carry

    lax.fori_loop(1, devices, tell, 0)
    home = pl.ds(pl.multiple_of(me * 8, 8), 8)
    note_in[home, :] = note_out[home, :]

    for c in range(3):
        disp_ref[c] = disp_in[c]
        vel_ref[c] = vel_in[c]
    scale_ref[...] = TIMESTEP / mass_ref[...]
    fill_tables(conn_ref, column_ref, pick_ref, back_ref, own_blocks, face_blocks)

    told = note_in.at[pl.ds(0, (devices - 1) * 8)]
    pltpu.make_async_copy(told, told, note_recv).wait()
    pltpu.make_async_copy(told, told, note_send).wait()
    heard = note_in[pl.ds(0, LANES, stride=8), :]
    heard_t = heard.T
    for s in range(steps):
        for r in range(2):
            q = 2 * s + r
            seers[s, r * LANES : (r + 1) * LANES, :] = one_hot(
                heard[:, q : q + 1] == (iota(square, 1) + 1).astype(F32)
            )
            seers_t[s, :, r * LANES : (r + 1) * LANES] = one_hot(
                heard_t[q : q + 1, :] == (iota(square, 0) + 1).astype(F32)
            )
    for copy in copies:
        copy.wait()

    surface = LANES
    groove = own_blocks - surface
    lane = iota(square, 1)

    def step(s, carry):
        cycle = [disp_ref[c][:, :surface].T for c in range(3)] + [vel_ref[0][:, :surface].T]
        mate = [disp_ref[c][:, groove:].T for c in range(3)] + [vel_ref[0][:, groove:].T]
        for c in range(3):
            face_out[c * 8 : c * 8 + 8, :] = cycle[c][:8]
            face_out[24 + c * 8 : 24 + c * 8 + 8, :] = mate[c][LANES - 8 :]
        faces = []
        for side, where in ((0, lower), (1, upper)):
            faces.append(
                pltpu.make_async_remote_copy(
                    src_ref=face_out.at[pl.ds(side * 24, 24)],
                    dst_ref=face_in.at[s, pl.ds((1 - side) * 24, 24)],
                    send_sem=face_send.at[s],
                    recv_sem=face_recv.at[s],
                    device_id=where,
                    device_id_type=MESH,
                )
            )
        for copy in faces:
            copy.start()
        mate[0] = mate[0] + clear_ref[...]

        for base, table, data in ((0, pickers, cycle), (8, seers, mate)):
            pieces = parts(jnp.concatenate(data, axis=1))
            packed = sum(dot(table[s], piece) for piece in pieces)
            for r in range(2):
                for k in range(4):
                    send_ref[pl.ds(base + r * 4 + k, LANES, stride=ROWS), :] = packed[
                        r * LANES : (r + 1) * LANES, k * LANES : (k + 1) * LANES
                    ]

        def ship(r, inner):
            other, where = peer(r)
            pltpu.make_async_remote_copy(
                src_ref=send_ref.at[pl.ds(pl.multiple_of(other * ROWS, ROWS), ROWS)],
                dst_ref=recv_ref.at[s, pl.ds(pl.multiple_of(me * ROWS, ROWS), ROWS)],
                send_sem=block_send.at[s],
                recv_sem=block_recv.at[s],
                device_id=where,
                device_id_type=MESH,
            ).start()
            return inner

        lax.fori_loop(1, devices, ship, 0)
        own_rows = pl.ds(pl.multiple_of(me * ROWS, ROWS), ROWS)
        recv_ref[s, own_rows, :] = send_ref[own_rows, :]

        for c in range(3):
            for p, piece in enumerate(parts(disp_ref[c])):
                state_ref[p, c * LANES : (c + 1) * LANES, :own_blocks] = piece
        both = face_in.at[s]
        pltpu.make_async_copy(both, both, face_recv.at[s]).wait()
        halo = padded_transpose(face_in[s])
        for c in range(3):
            turned = pltpu.roll(halo, LANES - 8 * c, 1) if c else halo
            for p, piece in enumerate(parts(turned)):
                state_ref[p, c * LANES : (c + 1) * LANES, own_blocks:] = piece

        gather_tiles(state_ref, pick_ref, tile_ref)

        def group_step(group, inner):
            element_group(group, stiff_ref, conn_ref, tile_ref, near_ref, spread_ref)
            return inner

        lax.fori_loop(0, groups, group_step, 0)
        force_ref[...] = sum(dot(spread_ref[p], back_ref[...]) for p in range(3))

        edge = jnp.zeros(square, F32)
        for c in range(3):
            tail = force_ref[c * LANES : (c + 1) * LANES, own_blocks:]
            turned = pltpu.roll(tail, 8 * c, 1) if c else tail
            here = ((lane >= 8 * c) & (lane < 8 * c + 8)) | (
                (lane >= 24 + 8 * c) & (lane < 32 + 8 * c)
            )
            edge = jnp.where(here, turned, edge)
        edge_out[...] = edge.T[:48]
        for side, where in ((0, lower), (1, upper)):
            pltpu.make_async_remote_copy(
                src_ref=edge_out.at[pl.ds(side * 24, 24)],
                dst_ref=edge_in.at[s, pl.ds((1 - side) * 24, 24)],
                send_sem=edge_send.at[s],
                recv_sem=edge_recv.at[s],
                device_id=where,
                device_id_type=MESH,
            ).start()

        arrived = recv_ref.at[s, pl.ds(0, (devices - 1) * ROWS)]
        pltpu.make_async_copy(arrived, arrived, block_recv.at[s]).wait()

        def rows_of(ref, base, r):
            return [ref[pl.ds(base + r * 4 + k, LANES, stride=ROWS), :] for k in range(4)]

        incoming = recv_ref.at[s]
        on_groove, on_cycle = [], []
        for r in range(2):
            on_groove.append(
                jnp.concatenate(
                    contact_terms(rows_of(incoming, 0, r), rows_of(send_ref, 8, r)), axis=1
                )
            )
            on_cycle.append(
                jnp.concatenate(
                    contact_terms(rows_of(send_ref, 0, r), rows_of(incoming, 8, r)), axis=1
                )
            )
        groove_force = sum(
            dot(seers_t[s], piece) for piece in parts(jnp.concatenate(on_groove, axis=0))
        )
        cycle_force = sum(
            dot(pickers_t[s], piece) for piece in parts(jnp.concatenate(on_cycle, axis=0))
        )

        both = edge_in.at[s]
        pltpu.make_async_copy(both, both, edge_recv.at[s]).wait()
        edge = padded_transpose(edge_in[s])
        for c in range(3):
            span = slice(c * LANES, (c + 1) * LANES)
            first = pltpu.roll(edge, LANES - 8 * c, 1) if c else edge
            last = pltpu.roll(edge, 96 - 8 * c, 1)
            extra = (
                -cycle_force[:, span].T - jnp.where(lane < 8, first, 0.0),
                None,
                groove_force[:, span].T - jnp.where(lane >= LANES - 8, last, 0.0),
            )
            for low, high, add in (
                (0, surface, extra[0]),
                (surface, groove, None),
                (groove, own_blocks, extra[2]),
            ):
                at = slice(low, high)
                pull = load_ref[c][:, at] - force_ref[span, at]
                if add is not None:
                    pull = pull + add
                speed = vel_ref[c, :, at] + pull * scale_ref[:, at]
                vel_ref[c, :, at] = speed
                disp_ref[c, :, at] = disp_ref[c, :, at] + TIMESTEP * speed

        sent = send_ref.at[pl.ds(0, (devices - 1) * ROWS)]
        pltpu.make_async_copy(sent, sent, block_send.at[s]).wait()
        pltpu.make_async_copy(face_out, face_out, face_send.at[s]).wait()
        pltpu.make_async_copy(edge_out, edge_out, edge_send.at[s]).wait()
        return carry

    lax.fori_loop(0, steps, step, 0)


def body(
    displacement, velocity, load, mass, stiffness, connectivity, clearance, match_device, match_slot
):
    steps = match_slot.shape[0]
    circ_count, xsec_count = lax.axis_size("circ"), lax.axis_size("xsec")
    devices = circ_count * xsec_count
    own_blocks = displacement.shape[1] // LANES
    face_blocks = FACE // LANES
    groups = stiffness.shape[2] // LANES
    wide = own_blocks + LANES

    def turned(array):
        return array.reshape(3, own_blocks, LANES).transpose(0, 2, 1)

    links = connectivity.reshape(WIDTH, groups, LANES).transpose(1, 0, 2)
    columns = connectivity[0].reshape(groups, LANES).T
    vm = pl.BlockSpec(memory_space=pltpu.VMEM)
    shape = jax.ShapeDtypeStruct((3, LANES, own_blocks), F32)
    dma = pltpu.SemaphoreType.DMA
    deform, motion = pl.pallas_call(
        functools.partial(kernel, (circ_count, xsec_count, steps, own_blocks, face_blocks)),
        out_shape=(shape, shape),
        in_specs=[vm, vm, vm, vm, pl.BlockSpec(memory_space=pl.ANY), vm, vm, vm, vm, vm],
        out_specs=(vm, vm),
        scratch_shapes=[
            pltpu.VMEM((groups, WIDTH, WIDTH, LANES), F32),
            pltpu.VMEM((wide, groups * LANES), BF16),
            pltpu.VMEM((groups * LANES, wide), BF16),
            pltpu.VMEM((groups, 3 * LANES, LANES), F32),
            pltpu.VMEM((3, WIDTH, LANES), F32),
            pltpu.VMEM((3, 3 * LANES, groups * LANES), BF16),
            pltpu.VMEM((3, 3 * LANES, wide), BF16),
            pltpu.VMEM((3 * LANES, wide), F32),
            pltpu.VMEM((LANES, own_blocks), F32),
            pltpu.VMEM((steps, 2 * LANES, LANES), BF16),
            pltpu.VMEM((steps, LANES, 2 * LANES), BF16),
            pltpu.VMEM((steps, 2 * LANES, LANES), BF16),
            pltpu.VMEM((steps, LANES, 2 * LANES), BF16),
            pltpu.VMEM((devices * 8, LANES), F32),
            pltpu.VMEM((devices * 8, LANES), F32),
            pltpu.VMEM((devices * ROWS, LANES), F32),
            pltpu.VMEM((steps, devices * ROWS, LANES), F32),
            pltpu.VMEM((48, LANES), F32),
            pltpu.VMEM((steps, 48, LANES), F32),
            pltpu.VMEM((48, LANES), F32),
            pltpu.VMEM((steps, 48, LANES), F32),
            dma((groups,)),
            dma,
            dma,
            dma((steps,)),
            dma((steps,)),
            dma((steps,)),
            dma((steps,)),
            dma((steps,)),
            dma((steps,)),
        ],
        compiler_params=pltpu.CompilerParams(
            collective_id=0, has_side_effects=True, vmem_limit_bytes=52 * 2**20
        ),
    )(
        turned(displacement),
        turned(velocity),
        turned(load),
        mass.reshape(own_blocks, LANES).T,
        stiffness,
        links,
        columns,
        clearance,
        match_device[:, :, 0],
        match_slot,
    )

    def restored(array):
        return array.transpose(0, 2, 1).reshape(3, own_blocks * LANES)

    return restored(deform), restored(motion)


def solution(mesh):
    return jax.shard_map(
        body,
        mesh=mesh,
        in_specs=(
            P(None, ("circ", "xsec")),
            P(None, ("circ", "xsec")),
            P(None, ("circ", "xsec")),
            P(("circ", "xsec")),
            P(None, None, ("circ", "xsec")),
            P(None, ("circ", "xsec")),
            P(("circ", "xsec"), None),
            P(None, ("circ", "xsec"), None),
            P(None, ("circ", "xsec")),
        ),
        out_specs=(P(None, ("circ", "xsec")), P(None, ("circ", "xsec"))),
        check_vma=False,
    )
```

time: 830 us -> 165 us (0.20); the launches traced: 817 us -> 165 us
  matrix products: 498 us -> 0 us
  starting transfers between devices: 151 us -> 0 us
  Pallas kernels: 0 us -> 150 us
  local copies, waits for them, and re-layouts: 108 us -> 14.2 us
  other arithmetic: 29.5 us -> 0 us
  waiting for transfers between devices: 28.5 us -> 0 us
    dot_general x36 -> x0, matrix products: 498 us -> none  [the longest x4 224 us: body(): jnp.einsum('ije,cje->cie', stiffness, gathered, precision=lax.Precision.H...]
    pallas_call x0 -> x1, Pallas kernels: none -> 150 us  [body(): pl.pallas_call(functools.partial(kernel, (circ_count, xsec_count, steps,...]
    all_to_all x12 -> x0, starting transfers between devices: 110 us -> none  [the longest x4 41 us: contact_step(): lax.all_to_all(pair_force, ('circ', 'xsec'), split_axis=0, concat_axis=0,...]
    ppermute x16 -> x0, starting transfers between devices: 40.8 us -> none  [the longest x4 21.6 us: with_halo(): lax.ppermute(lax.slice_in_dim(block, 0, width, axis=dim), axis, backward)]
    unnamed x93 -> x9, local copies, waits for them, and re-layouts: 37.2 us -> 5.72 us
    all_to_all x12 -> x0, waiting for transfers between devices: 28.4 us -> none  [the longest x4 28.4 us: contact_step(): lax.all_to_all(pair_force, ('circ', 'xsec'), split_axis=0, concat_axis=0,...]
    dot_general x8 -> x0, local copies, waits for them, and re-layouts: 13.4 us -> none  [the longest x4 8.88 us: body(): jnp.einsum('et,ctm->cme', tile_pick, tiles, precision=lax.Precision.HIGHEST)]
    slice x34 -> x1, local copies, waits for them, and re-layouts: 14 us -> 0.76 us  [body(): columns = connectivity[0].reshape(groups, LANES).T]
  transfers between devices with their start and end apart: 28 -> 0, of which waited for: 4 -> 0; matrix products, arithmetic and copies ran while one was open for 74% -> 0% of each run, Pallas kernels for 0% -> 0%
where the time goes in v1:
time: 165 us
  Pallas kernels  150 us (91%)
  local copies, waits for them, and re-layouts  14.2 us (9%)
    pallas_call x1, Pallas kernels, body(): pl.pallas_call(functools.partial(kernel, (circ_count, xsec_count, steps,...  150 us
    unnamed x9, local copies, waits for them, and re-layouts  5.72 us

profile of v1, /device:TPU:36, one launch (start us, length us, event | category | flops | bytes accessed | tf_op | source)
XLA Modules:
  0.0 164.6 jit_solution(16120212510343188798)
XLA Ops:
  0.6 0.8 slice.3
  1.4 0.1 copy.16
  1.5 1.1 copy.14
  2.6 1.0 bitcast_bitcast_fusion.conn_ref
  3.5 1.2 copy.33
  4.7 1.1 copy.11
  5.8 1.2 copy.32
  6.9 1.1 copy.12
  8.0 1.2 copy.31
  9.2 1.1 copy.13
  10.2 0.0 copy-start
  10.2 0.8 copy-done
  11.1 0.0 copy-start.1
  11.1 0.7 copy-done.1
  11.7 0.0 copy-start.2
  11.7 0.7 copy-done.2
  12.4 149.7 %shard_map.104 = (f32[3,128,384]{2,1,0:T(8,128)S(1)}, f32[3,128,384]{2,1,0:T(8,128)S(1)}) custom-call(f32[3,128,384]{2,1,0:T(8,128)} %bitcast.45, f32[3,128,384]{2,1,0:T(8,128)} %bitcast.46, f32[3,128,384]{2,1,0:T(8,128)} %bitcast.47, f32[128,384]{1,0:T(8,128)S(1)} %bitcast.35, f32[64,64,1024]{2,1,0:T(8,128)} %stiff_hbm.1, ...), custom_call_target="tpu_custom_call" | custom-call | tf_op jit(solution)/shard_map/pallas_call | solution.py:398
  162.1 0.2 copy.17
  162.4 0.2 copy.18
  162.6 2.0 %copy_bitcast_fusion = (f32[3,49152]{1,0:T(4,128)}, f32[3,49152]{1,0:T(4,128)}) fusion(f32[1,3,384,128]{3,2,1,0:T(8,128)S(1)} %bitcast.41, f32[1,3,384,128]{3,2,1,0:T(8,128)S(1)} %bitcast.40), kind=kLoop, calls=%fused_computation | loop fusion | bytes 2359296 | tf_op jit(solution)/shard_map/reshape | solution.py:452
Async XLA Ops:
  10.2 0.8 copy-start
  11.1 0.7 copy-start.1
  11.7 0.7 copy-start.2

commit v2 on v1

--- a/solution.py
+++ b/solution.py
@@ -28,6 +28,11 @@
     return first, second, third
 
 
+def halves(x):
+    first = x.astype(BF16)
+    return first, (x - first.astype(F32)).astype(BF16)
+
+
 def one_hot(mask):
     return jnp.where(mask, 1.0, 0.0).astype(BF16)
 
@@ -65,13 +70,13 @@
     )
 
 
-def fill_tables(conn_ref, column_ref, pick_ref, back_ref, own_blocks, face_blocks):
-    groups = conn_ref.shape[0]
+def fill_tables(conn_ref, pick_ref, back_ref, own_blocks, face_blocks):
+    groups = conn_ref.shape[1] // LANES
     columns = pick_ref.shape[0]
     for group in range(groups):
-        row = column_of(conn_ref[group, 0:1, :] >> 7, own_blocks, face_blocks)
+        row = column_of(conn_ref[0:1, group * LANES : (group + 1) * LANES] >> 7, own_blocks, face_blocks)
         pick_ref[:, group * LANES : (group + 1) * LANES] = one_hot(iota((columns, LANES), 0) == row)
-        col = column_of(column_ref[:, group : group + 1] >> 7, own_blocks, face_blocks)
+        col = jnp.broadcast_to(row, (LANES, LANES)).astype(F32).T[:, :1].astype(jnp.int32)
         back_ref[group * LANES : (group + 1) * LANES, :] = one_hot(iota((LANES, columns), 1) == col)
 
 
@@ -79,7 +84,7 @@
     groups = tile_ref.shape[0]
     for pair in range(groups // 2):
         pick = pick_ref[:, pair * 256 : (pair + 1) * 256]
-        found = sum(dot(state_ref[p], pick) for p in range(3))
+        found = dot(state_ref[0], pick) + dot(state_ref[1], pick)
         tile_ref[2 * pair] = found[:, :LANES]
         tile_ref[2 * pair + 1] = found[:, LANES:]
 
@@ -116,22 +121,22 @@
         return tuple(out)
 
     zero = jnp.zeros((WIDTH, LANES), F32)
-    sums = lax.fori_loop(0, WIDTH, row, (zero, zero, zero))
+    sums = lax.fori_loop(0, WIDTH, row, (zero, zero, zero), unroll=8)
     at = pl.ds(pl.multiple_of(group * LANES, LANES), LANES)
     for c in range(3):
         for half in range(2):
             kept = jnp.where(odd if half else jnp.logical_not(odd), sums[c], 0.0)
-            for p, part in enumerate(parts(kept)):
+            for p, part in enumerate(halves(kept)):
                 spread_ref[p, c * 128 + half * 64 : c * 128 + half * 64 + 64, at] = part
 
 
 def kernel(
-    counts, disp_in, vel_in, load_ref, mass_ref, stiff_hbm, conn_ref, column_ref, clear_ref,
-    target_ref, slot_ref, disp_ref, vel_ref,
-    stiff_ref, pick_ref, back_ref, tile_ref, near_ref, spread_ref, state_ref, force_ref, scale_ref,
+    counts, disp_in, vel_in, load_in, mass_ref, stiff_hbm, conn_ref, clear_ref,
+    target_ref, slot_ref, disp_out, vel_out,
+    disp_ref, vel_ref, load_ref, given_ref, link_ref, stiff_ref, pick_ref, back_ref, tile_ref, near_ref, spread_ref, state_ref, force_ref, scale_ref,
     pickers, pickers_t, seers, seers_t, note_out, note_in, send_ref, recv_ref,
     face_out, face_in, edge_out, edge_in,
-    stiff_sem, note_send, note_recv, block_send, block_recv, face_send, face_recv, edge_send,
+    given_sem, stiff_sem, note_send, note_recv, block_send, block_recv, face_send, face_recv, edge_send,
     edge_recv,
 ):
     circ_count, xsec_count, steps, own_blocks, face_blocks = counts
@@ -146,6 +151,12 @@
         other = lax.rem(me + r, devices)
         return other, (other // xsec_count, lax.rem(other, xsec_count))
 
+    given = [
+        pltpu.make_async_copy(source, given_ref.at[i], given_sem.at[i])
+        for i, source in enumerate((disp_in, vel_in, load_in))
+    ]
+    for copy in given:
+        copy.start()
     copies = [
         pltpu.make_async_copy(
             stiff_hbm.at[:, :, pl.ds(g * LANES, LANES)], stiff_ref.at[g], stiff_sem.at[g]
@@ -166,7 +177,7 @@
     square = (LANES, LANES)
     note = jnp.zeros(square, F32)
     for s in range(steps):
-        dev_row = target_ref[s : s + 1, :]
+        dev_row = target_ref[s]
         dev_square = jnp.broadcast_to(dev_row, square)
         dev_col = dev_square.astype(F32).T.astype(jnp.int32)
         earlier = (dev_col == dev_square) & (iota(square, 0) < iota(square, 1))
@@ -185,6 +196,12 @@
     note_out[...] = jnp.zeros(note_out.shape, F32)
     note_out[pl.ds(0, LANES, stride=8), :] = note
 
+    for i, ref in enumerate((disp_ref, vel_ref, load_ref)):
+        given[i].wait()
+        for c in range(3):
+            ref[c] = given_ref[i, :, c, :].T
+    scale_ref[...] = TIMESTEP / mass_ref[...].T
+
     pl.semaphore_wait(barrier, devices - 1)
 
     def tell(r, carry):
@@ -203,11 +220,9 @@
     home = pl.ds(pl.multiple_of(me * 8, 8), 8)
     note_in[home, :] = note_out[home, :]
 
-    for c in range(3):
-        disp_ref[c] = disp_in[c]
-        vel_ref[c] = vel_in[c]
-    scale_ref[...] = TIMESTEP / mass_ref[...]
-    fill_tables(conn_ref, column_ref, pick_ref, back_ref, own_blocks, face_blocks)
+    for group in range(groups):
+        link_ref[group] = conn_ref[:, group * LANES : (group + 1) * LANES]
+    fill_tables(conn_ref, pick_ref, back_ref, own_blocks, face_blocks)
 
     told = note_in.at[pl.ds(0, (devices - 1) * 8)]
     pltpu.make_async_copy(told, told, note_recv).wait()
@@ -278,28 +293,30 @@
         recv_ref[s, own_rows, :] = send_ref[own_rows, :]
 
         for c in range(3):
-            for p, piece in enumerate(parts(disp_ref[c])):
+            for p, piece in enumerate(halves(disp_ref[c])):
                 state_ref[p, c * LANES : (c + 1) * LANES, :own_blocks] = piece
         both = face_in.at[s]
         pltpu.make_async_copy(both, both, face_recv.at[s]).wait()
         halo = padded_transpose(face_in[s])
         for c in range(3):
             turned = pltpu.roll(halo, LANES - 8 * c, 1) if c else halo
-            for p, piece in enumerate(parts(turned)):
+            for p, piece in enumerate(halves(turned)):
                 state_ref[p, c * LANES : (c + 1) * LANES, own_blocks:] = piece
 
         gather_tiles(state_ref, pick_ref, tile_ref)
 
         def group_step(group, inner):
-            element_group(group, stiff_ref, conn_ref, tile_ref, near_ref, spread_ref)
+            element_group(group, stiff_ref, link_ref, tile_ref, near_ref, spread_ref)
             return inner
 
         lax.fori_loop(0, groups, group_step, 0)
-        force_ref[...] = sum(dot(spread_ref[p], back_ref[...]) for p in range(3))
+        tails = dot(spread_ref[0], back_ref[:, own_blocks:]) + dot(
+            spread_ref[1], back_ref[:, own_blocks:]
+        )
 
         edge = jnp.zeros(square, F32)
         for c in range(3):
-            tail = force_ref[c * LANES : (c + 1) * LANES, own_blocks:]
+            tail = tails[c * LANES : (c + 1) * LANES]
             turned = pltpu.roll(tail, 8 * c, 1) if c else tail
             here = ((lane >= 8 * c) & (lane < 8 * c + 8)) | (
                 (lane >= 24 + 8 * c) & (lane < 32 + 8 * c)
@@ -316,6 +333,9 @@
                 device_id_type=MESH,
             ).start()
 
+        force_ref[...] = dot(spread_ref[0], back_ref[:, :own_blocks]) + dot(
+            spread_ref[1], back_ref[:, :own_blocks]
+        )
         arrived = recv_ref.at[s, pl.ds(0, (devices - 1) * ROWS)]
         pltpu.make_async_copy(arrived, arrived, block_recv.at[s]).wait()
 
@@ -374,6 +394,9 @@
         return carry
 
     lax.fori_loop(0, steps, step, 0)
+    for c in range(3):
+        disp_out[:, c, :] = disp_ref[c].T
+        vel_out[:, c, :] = vel_ref[c].T
 
 
 def body(
@@ -388,27 +411,31 @@
     wide = own_blocks + LANES
 
     def turned(array):
-        return array.reshape(3, own_blocks, LANES).transpose(0, 2, 1)
-
-    links = connectivity.reshape(WIDTH, groups, LANES).transpose(1, 0, 2)
-    columns = connectivity[0].reshape(groups, LANES).T
+        return array.reshape(3, own_blocks, LANES).transpose(1, 0, 2)
+
     vm = pl.BlockSpec(memory_space=pltpu.VMEM)
-    shape = jax.ShapeDtypeStruct((3, LANES, own_blocks), F32)
+    far = pl.BlockSpec(memory_space=pl.ANY)
+    shape = jax.ShapeDtypeStruct((own_blocks, 3, LANES), F32)
     dma = pltpu.SemaphoreType.DMA
     deform, motion = pl.pallas_call(
         functools.partial(kernel, (circ_count, xsec_count, steps, own_blocks, face_blocks)),
         out_shape=(shape, shape),
-        in_specs=[vm, vm, vm, vm, pl.BlockSpec(memory_space=pl.ANY), vm, vm, vm, vm, vm],
+        in_specs=[far, far, far, vm, far, vm, vm, vm, vm],
         out_specs=(vm, vm),
         scratch_shapes=[
+            pltpu.VMEM((3, LANES, own_blocks), F32),
+            pltpu.VMEM((3, LANES, own_blocks), F32),
+            pltpu.VMEM((3, LANES, own_blocks), F32),
+            pltpu.VMEM((3, own_blocks, 3, LANES), F32),
+            pltpu.VMEM((groups, WIDTH, LANES), jnp.int32),
             pltpu.VMEM((groups, WIDTH, WIDTH, LANES), F32),
             pltpu.VMEM((wide, groups * LANES), BF16),
             pltpu.VMEM((groups * LANES, wide), BF16),
             pltpu.VMEM((groups, 3 * LANES, LANES), F32),
             pltpu.VMEM((3, WIDTH, LANES), F32),
-            pltpu.VMEM((3, 3 * LANES, groups * LANES), BF16),
-            pltpu.VMEM((3, 3 * LANES, wide), BF16),
-            pltpu.VMEM((3 * LANES, wide), F32),
+            pltpu.VMEM((2, 3 * LANES, groups * LANES), BF16),
+            pltpu.VMEM((2, 3 * LANES, wide), BF16),
+            pltpu.VMEM((3 * LANES, own_blocks), F32),
             pltpu.VMEM((LANES, own_blocks), F32),
             pltpu.VMEM((steps, 2 * LANES, LANES), BF16),
             pltpu.VMEM((steps, LANES, 2 * LANES), BF16),
@@ -422,6 +449,7 @@
             pltpu.VMEM((steps, 48, LANES), F32),
             pltpu.VMEM((48, LANES), F32),
             pltpu.VMEM((steps, 48, LANES), F32),
+            dma((3,)),
             dma((groups,)),
             dma,
             dma,
@@ -433,23 +461,22 @@
             dma((steps,)),
         ],
         compiler_params=pltpu.CompilerParams(
-            collective_id=0, has_side_effects=True, vmem_limit_bytes=52 * 2**20
+            collective_id=0, has_side_effects=True, vmem_limit_bytes=62 * 2**20
         ),
     )(
         turned(displacement),
         turned(velocity),
         turned(load),
-        mass.reshape(own_blocks, LANES).T,
+        mass.reshape(own_blocks, LANES),
         stiffness,
-        links,
-        columns,
+        connectivity,
         clearance,
-        match_device[:, :, 0],
+        match_device.transpose(0, 2, 1),
         match_slot,
     )
 
     def restored(array):
-        return array.transpose(0, 2, 1).reshape(3, own_blocks * LANES)
+        return array.transpose(1, 0, 2).reshape(3, own_blocks * LANES)
 
     return restored(deform), restored(motion)
 

time: 165 us -> 127 us (0.77)
  Pallas kernels: 150 us -> 121 us
  local copies, waits for them, and re-layouts: 14.2 us -> 4.3 us
    pallas_call x1, Pallas kernels: 150 us -> 121 us  [body(): pl.pallas_call(functools.partial(kernel, (circ_count, xsec_count, steps,...]
    reshape x5 -> x0, local copies, waits for them, and re-layouts: 6.17 us -> none  [the longest x3 3.17 us: turned(): return array.reshape(3, own_blocks, LANES).transpose(0, 2, 1)]
    unnamed x9 -> x2, local copies, waits for them, and re-layouts: 5.72 us -> 4.3 us
where the time goes in v2:
time: 127 us; the launch traced here: 126 us
  Pallas kernels  121 us (95%)
  local copies, waits for them, and re-layouts  4.3 us (3%)
    pallas_call x1, Pallas kernels, body(): pl.pallas_call(functools.partial(kernel, (circ_count, xsec_count, steps,...  121 us
    unnamed x2, local copies, waits for them, and re-layouts  4.3 us

profile of v2, /device:TPU:36, one launch (start us, length us, event | category | flops | bytes accessed | tf_op | source)
XLA Modules:
  0.0 125.7 jit_solution(5721324971110108058)
XLA Ops:
  0.6 120.8 %shard_map.104 = (f32[384,3,128]{2,1,0:T(4,128)}, f32[384,3,128]{2,1,0:T(4,128)}) custom-call(f32[384,3,128]{2,1,0:T(4,128)} %bitcast.19, f32[384,3,128]{2,1,0:T(4,128)} %bitcast.20, f32[384,3,128]{2,1,0:T(4,128)} %bitcast.21, f32[384,128]{1,0:T(8,128)} %bitcast.22, f32[64,64,1024]{2,1,0:T(8,128)} %stiff_hbm.1, s32[64,1024]{1,0:T(8,128)} %conn_ref.1, ...), custom_call_target="tpu_custom_call" | custom-call | tf_op jit(solution)/shard_map/pallas_call | solution.py:420
  121.4 2.1 %copy.13 = f32[3,49152]{1,0:T(4,128)} copy(f32[3,49152]{1,0:T(4,128)} %bitcast.18) | data formatting | bytes 1179648
  123.5 2.1 %copy.14 = f32[3,49152]{1,0:T(4,128)} copy(f32[3,49152]{1,0:T(4,128)} %bitcast.17) | data formatting | bytes 1179648

commit v3 on v2

--- a/solution.py
+++ b/solution.py
@@ -89,43 +89,90 @@
         tile_ref[2 * pair + 1] = found[:, LANES:]
 
 
-def element_group(group, stiff_ref, conn_ref, tile_ref, near_ref, spread_ref):
-    links = conn_ref[group]
+def pick_rows(table, index):
+    out = []
+    for j in range(0, WIDTH, 8):
+        low = index[j : j + 8] & 7
+        high = index[j : j + 8] >> 3
+        value = jnp.take_along_axis(table[0:8], low, axis=0, mode="promise_in_bounds")
+        for m in range(1, WIDTH // 8):
+            other = jnp.take_along_axis(
+                table[m * 8 : m * 8 + 8], low, axis=0, mode="promise_in_bounds"
+            )
+            value = jnp.where(high == m, other, value)
+        out.append(value)
+    return jnp.concatenate(out, axis=0)
+
+
+def running_sums(rows):
+    at = iota((8, LANES), 0)
+    base = jnp.zeros((1, LANES), F32)
+    out = []
+    for j in range(0, WIDTH, 8):
+        piece = rows[j : j + 8]
+        for by in (1, 2, 4):
+            piece = piece + jnp.where(at >= by, pltpu.roll(piece, by, 0), 0.0)
+        piece = piece + base
+        base = piece[7:8]
+        out.append(piece)
+    return jnp.concatenate(out, axis=0)
+
+
+def sort_links(group, link_ref, key_ref, order_ref, end_ref):
+    at = iota((WIDTH, LANES), 0)
+    local = link_ref[group] & 63
+    keys = local * WIDTH + at
+    key_ref[...] = keys
+
+    def count(i, carry):
+        place, end = carry
+        key = key_ref[pl.ds(i, 1), :]
+        place = place + jnp.where(key < keys, 1, 0)
+        end = end + jnp.where(key < (at + 1) * WIDTH, 1, 0)
+        return place, end
+
+    zero = jnp.zeros((WIDTH, LANES), jnp.int32)
+    place, end = lax.fori_loop(0, WIDTH, count, (zero, zero), unroll=4)
+    end_ref[group] = end
+    key_ref[...] = place
+
+    def invert(i, order):
+        return jnp.where(key_ref[pl.ds(i, 1), :] == at, i, order)
+
+    order_ref[group] = lax.fori_loop(0, WIDTH, invert, zero, unroll=4)
+
+
+def element_group(group, stiff_ref, link_ref, order_ref, end_ref, tile_ref, row_ref, spread_ref):
+    links = link_ref[group]
     odd = ((links[0:1, :] >> 6) & 1) == 1
-    low = links & 7
-    high = (links >> 3) & 7
+    local = links & 63
+    near = []
     for c in range(3):
         tile = jnp.where(
             odd,
             tile_ref[group, c * 128 + 64 : c * 128 + 128, :],
             tile_ref[group, c * 128 : c * 128 + 64, :],
         )
-        for j in range(8):
-            index = low[j * 8 : j * 8 + 8]
-            which = high[j * 8 : j * 8 + 8]
-            value = jnp.take_along_axis(tile[0:8], index, axis=0, mode="promise_in_bounds")
-            for m in range(1, 8):
-                other = jnp.take_along_axis(
-                    tile[m * 8 : m * 8 + 8], index, axis=0, mode="promise_in_bounds"
-                )
-                value = jnp.where(which == m, other, value)
-            near_ref[c, j * 8 : j * 8 + 8, :] = value
-
-    def row(i, sums):
+        near.append(pick_rows(tile, local))
+
+    def row(i, carry):
         stiff = stiff_ref[group, i]
-        hit = iota((WIDTH, LANES), 0) == (conn_ref[group, pl.ds(i, 1), :] & 63)
-        out = []
-        for c in range(3):
-            force = jnp.sum(stiff * near_ref[c], axis=0, keepdims=True)
-            out.append(sums[c] + jnp.where(hit, force, 0.0))
-        return tuple(out)
-
-    zero = jnp.zeros((WIDTH, LANES), F32)
-    sums = lax.fori_loop(0, WIDTH, row, (zero, zero, zero), unroll=8)
+        for c in range(3):
+            row_ref[c, pl.ds(i, 1), :] = jnp.sum(stiff * near[c], axis=0, keepdims=True)
+        return carry
+
+    lax.fori_loop(0, WIDTH, row, 0, unroll=8)
+    order = order_ref[group]
+    end = end_ref[group]
+    last = jnp.maximum(end - 1, 0)
     at = pl.ds(pl.multiple_of(group * LANES, LANES), LANES)
     for c in range(3):
+        totals = pick_rows(running_sums(pick_rows(row_ref[c], order)), last)
+        totals = jnp.where(end > 0, totals, 0.0)
+        before = jnp.where(iota((WIDTH, LANES), 0) > 0, pltpu.roll(totals, 1, 0), 0.0)
+        sums = totals - before
         for half in range(2):
-            kept = jnp.where(odd if half else jnp.logical_not(odd), sums[c], 0.0)
+            kept = jnp.where(odd if half else jnp.logical_not(odd), sums, 0.0)
             for p, part in enumerate(halves(kept)):
                 spread_ref[p, c * 128 + half * 64 : c * 128 + half * 64 + 64, at] = part
 
@@ -133,7 +180,7 @@
 def kernel(
     counts, disp_in, vel_in, load_in, mass_ref, stiff_hbm, conn_ref, clear_ref,
     target_ref, slot_ref, disp_out, vel_out,
-    disp_ref, vel_ref, load_ref, given_ref, link_ref, stiff_ref, pick_ref, back_ref, tile_ref, near_ref, spread_ref, state_ref, force_ref, scale_ref,
+    disp_ref, vel_ref, load_ref, given_ref, key_ref, order_ref, end_ref, link_ref, stiff_ref, pick_ref, back_ref, tile_ref, near_ref, spread_ref, state_ref, force_ref, scale_ref,
     pickers, pickers_t, seers, seers_t, note_out, note_in, send_ref, recv_ref,
     face_out, face_in, edge_out, edge_in,
     given_sem, stiff_sem, note_send, note_recv, block_send, block_recv, face_send, face_recv, edge_send,
@@ -224,6 +271,12 @@
         link_ref[group] = conn_ref[:, group * LANES : (group + 1) * LANES]
     fill_tables(conn_ref, pick_ref, back_ref, own_blocks, face_blocks)
 
+    def sort_step(group, carry):
+        sort_links(group, link_ref, key_ref, order_ref, end_ref)
+        return carry
+
+    lax.fori_loop(0, groups, sort_step, 0)
+
     told = note_in.at[pl.ds(0, (devices - 1) * 8)]
     pltpu.make_async_copy(told, told, note_recv).wait()
     pltpu.make_async_copy(told, told, note_send).wait()
@@ -306,7 +359,9 @@
         gather_tiles(state_ref, pick_ref, tile_ref)
 
         def group_step(group, inner):
-            element_group(group, stiff_ref, link_ref, tile_ref, near_ref, spread_ref)
+            element_group(
+                group, stiff_ref, link_ref, order_ref, end_ref, tile_ref, near_ref, spread_ref
+            )
             return inner
 
         lax.fori_loop(0, groups, group_step, 0)
@@ -395,8 +450,16 @@
 
     lax.fori_loop(0, steps, step, 0)
     for c in range(3):
-        disp_out[:, c, :] = disp_ref[c].T
-        vel_out[:, c, :] = vel_ref[c].T
+        given_ref[0, :, c, :] = disp_ref[c].T
+        given_ref[1, :, c, :] = vel_ref[c].T
+    back = [
+        pltpu.make_async_copy(given_ref.at[i], out, given_sem.at[i])
+        for i, out in enumerate((disp_out, vel_out))
+    ]
+    for copy in back:
+        copy.start()
+    for copy in back:
+        copy.wait()
 
 
 def body(
@@ -421,12 +484,15 @@
         functools.partial(kernel, (circ_count, xsec_count, steps, own_blocks, face_blocks)),
         out_shape=(shape, shape),
         in_specs=[far, far, far, vm, far, vm, vm, vm, vm],
-        out_specs=(vm, vm),
+        out_specs=(far, far),
         scratch_shapes=[
             pltpu.VMEM((3, LANES, own_blocks), F32),
             pltpu.VMEM((3, LANES, own_blocks), F32),
             pltpu.VMEM((3, LANES, own_blocks), F32),
             pltpu.VMEM((3, own_blocks, 3, LANES), F32),
+            pltpu.VMEM((WIDTH, LANES), jnp.int32),
+            pltpu.VMEM((groups, WIDTH, LANES), jnp.int32),
+            pltpu.VMEM((groups, WIDTH, LANES), jnp.int32),
             pltpu.VMEM((groups, WIDTH, LANES), jnp.int32),
             pltpu.VMEM((groups, WIDTH, WIDTH, LANES), F32),
             pltpu.VMEM((wide, groups * LANES), BF16),

time: 127 us -> 113 us (0.89)
  the two profiles are of different devices: /device:TPU:36 before, /device:TPU:0 now
where the time goes in v3:
time: 113 us
  Pallas kernels  108 us (96%)
  local copies, waits for them, and re-layouts  4.3 us (4%)
    pallas_call x1, Pallas kernels, body(): pl.pallas_call(functools.partial(kernel, (circ_count, xsec_count, steps,...  108 us
    unnamed x2, local copies, waits for them, and re-layouts  4.3 us

profile of v3, /device:TPU:0, one launch (start us, length us, event | category | flops | bytes accessed | tf_op | source)
XLA Modules:
  0.0 113.2 jit_solution(17206152176383962666)
XLA Ops:
  0.6 108.3 %shard_map.104 = (f32[384,3,128]{2,1,0:T(4,128)}, f32[384,3,128]{2,1,0:T(4,128)}) custom-call(f32[384,3,128]{2,1,0:T(4,128)} %bitcast.19, f32[384,3,128]{2,1,0:T(4,128)} %bitcast.20, f32[384,3,128]{2,1,0:T(4,128)} %bitcast.21, f32[384,128]{1,0:T(8,128)} %bitcast.22, f32[64,64,1024]{2,1,0:T(8,128)} %stiff_hbm.1, s32[64,1024]{1,0:T(8,128)} %conn_ref.1, ...), custom_call_target="tpu_custom_call" | custom-call | tf_op jit(solution)/shard_map/pallas_call | solution.py:483
  108.9 2.1 %copy.13 = f32[3,49152]{1,0:T(4,128)} copy(f32[3,49152]{1,0:T(4,128)} %bitcast.18) | data formatting | bytes 1179648
  111.1 2.1 %copy.14 = f32[3,49152]{1,0:T(4,128)} copy(f32[3,49152]{1,0:T(4,128)} %bitcast.17) | data formatting | bytes 1179648

commit v4 on v3

--- a/solution.py
+++ b/solution.py
@@ -18,14 +18,6 @@
 BF16 = jnp.bfloat16
 F32 = jnp.float32
 MESH = pl.DeviceIdType.MESH
-
-
-def parts(x):
-    first = x.astype(BF16)
-    rest = x - first.astype(F32)
-    second = rest.astype(BF16)
-    third = (rest - second.astype(F32)).astype(BF16)
-    return first, second, third
 
 
 def halves(x):
@@ -321,7 +313,7 @@
         mate[0] = mate[0] + clear_ref[...]
 
         for base, table, data in ((0, pickers, cycle), (8, seers, mate)):
-            pieces = parts(jnp.concatenate(data, axis=1))
+            pieces = halves(jnp.concatenate(data, axis=1))
             packed = sum(dot(table[s], piece) for piece in pieces)
             for r in range(2):
                 for k in range(4):
@@ -411,10 +403,10 @@
                 )
             )
         groove_force = sum(
-            dot(seers_t[s], piece) for piece in parts(jnp.concatenate(on_groove, axis=0))
+            dot(seers_t[s], piece) for piece in halves(jnp.concatenate(on_groove, axis=0))
         )
         cycle_force = sum(
-            dot(pickers_t[s], piece) for piece in parts(jnp.concatenate(on_cycle, axis=0))
+            dot(pickers_t[s], piece) for piece in halves(jnp.concatenate(on_cycle, axis=0))
         )
 
         both = edge_in.at[s]

time: 113 us -> 111 us (0.982)
  the two profiles are of different devices: /device:TPU:0 before, /device:TPU:63 now
where the time goes in v4:
time: 111 us
  Pallas kernels  106 us (95%)
  local copies, waits for them, and re-layouts  4.3 us (4%)
    pallas_call x1, Pallas kernels, body(): pl.pallas_call(functools.partial(kernel, (circ_count, xsec_count, steps,...  106 us
    unnamed x2, local copies, waits for them, and re-layouts  4.3 us

profile of v4, /device:TPU:63, one launch (start us, length us, event | category | flops | bytes accessed | tf_op | source)
XLA Modules:
  0.0 110.5 jit_solution(4526841365764850771)
XLA Ops:
  0.6 105.6 %shard_map.104 = (f32[384,3,128]{2,1,0:T(4,128)}, f32[384,3,128]{2,1,0:T(4,128)}) custom-call(f32[384,3,128]{2,1,0:T(4,128)} %bitcast.19, f32[384,3,128]{2,1,0:T(4,128)} %bitcast.20, f32[384,3,128]{2,1,0:T(4,128)} %bitcast.21, f32[384,128]{1,0:T(8,128)} %bitcast.22, f32[64,64,1024]{2,1,0:T(8,128)} %stiff_hbm.1, s32[64,1024]{1,0:T(8,128)} %conn_ref.1, ...), custom_call_target="tpu_custom_call" | custom-call | tf_op jit(solution)/shard_map/pallas_call | solution.py:475
  106.2 2.1 %copy.13 = f32[3,49152]{1,0:T(4,128)} copy(f32[3,49152]{1,0:T(4,128)} %bitcast.18) | data formatting | bytes 1179648
  108.4 2.1 %copy.14 = f32[3,49152]{1,0:T(4,128)} copy(f32[3,49152]{1,0:T(4,128)} %bitcast.17) | data formatting | bytes 1179648
